TPU v7x, 128 devices: a whole 4x4x4 slice. The times are simulated.
128 devices in a mesh: gr: 8 (over y_hi, z), gc: 16 (over x, y_lo, core).
Axes of the slice: x: 4, y: 4 (y_hi: 2, y_lo: 2; y = y_hi * 2 + y_lo), z: 4, core: 2. Of those that a mesh axis runs over, the one named last changes fastest.
Arguments:
- items: bfloat16 [16384, 4096], P(('gr', 'gc'))
- position_of: int32 [16384], P(('gr', 'gc')), may hold values from 0 to 16383, as said below
Outputs:
- similarity: bfloat16 [16384, 16384], P('gr', 'gc')
- best_other: float32 [16384], P('gr')
Inputs may be any that keep to these rules, and one draw needn't show every extreme that they name: `position_of`: A permutation. Position p has home device p // 128 in the order gr+gc; the items of device s go to home devices s * 128, s * 128 + 1, ... taken modulo 128, so each device sends at most 1 items to each home device and each home device receives 128.
All inputs are finite; a program needn't handle non-finite values.
Results may differ from a plain program's by a relative error of at most 0.001.
Values may be sent and summed in bfloat16 or wider, within the bound.
No kernel may reach another device: no remote copies, remote signals or barrier semaphores. Data moves between devices by JAX's collectives and lax.ppermute only.
A program may use at most 128 MiB of HBM per device.

v0:
```python
import jax
import jax.numpy as jnp
from jax import lax
from jax.sharding import PartitionSpec as P


def inverse_norm(block):
    wide = block.astype(jnp.float32)
    return 1.0 / jnp.sqrt(jnp.sum(wide * wide, axis=1) + 1e-06)


def per_device(items, position_of):
    count = items.shape[0]
    width = items.shape[1]
    n_rows = lax.axis_size("gr")
    n_cols = lax.axis_size("gc")
    shards = n_rows * n_cols
    slots = (count + shards - 1) // shards
    dest = position_of // count
    earlier = (dest[None, :] == dest[:, None]) & (position_of[None, :] < position_of[:, None])
    rank = jnp.sum(earlier.astype(jnp.int32), axis=1)
    slot = dest * slots + rank
    send = jnp.zeros((shards * slots, width), items.dtype).at[slot].set(items)
    send_pos = jnp.full((shards * slots,), -1, jnp.int32).at[slot].set(position_of)
    arrived, arrived_pos = (
        lax.all_to_all(send, ("gr", "gc"), split_axis=0, concat_axis=0, tiled=True),
        lax.all_to_all(send_pos, ("gr", "gc"), split_axis=0, concat_axis=0, tiled=True),
    )
    target = jnp.where(arrived_pos >= 0, arrived_pos % count, count)
    local = jnp.zeros_like(items).at[target].set(arrived, mode="drop")
    rows = lax.all_gather(local, "gc", axis=0, tiled=True)
    row_inv = inverse_norm(rows)
    piece = lax.all_gather(local, "gr", axis=0, tiled=True)
    product = lax.dot_general(
        rows, piece, (((1,), (1,)), ((), ())), preferred_element_type=jnp.float32
    )
    scaled = product * row_inv[:, None] * inverse_norm(piece)[None, :]
    row_here = lax.axis_index("gr")
    col_here = lax.axis_index("gc")
    row_local = jnp.arange(count * n_cols, dtype=jnp.int32)[:, None]
    col_local = jnp.arange(count * n_rows, dtype=jnp.int32)[None, :]
    itself = (row_local == col_here * count + col_local % count) & (col_local // count == row_here)
    masked = jnp.where(itself, jnp.float32(-2.0), scaled)
    best = lax.pmax(jnp.max(masked, axis=1), "gc")
    return (scaled.astype(jnp.bfloat16), best)


def solution(mesh):
    return jax.shard_map(
        per_device,
        mesh=mesh,
        in_specs=(P(("gr", "gc"), None), P(("gr", "gc"))),
        out_specs=(P("gr", "gc"), P("gr")),
        check_vma=False,
    )
```

profile of v0, /device:TPU:0, one launch (start us, length us, event | category | flops | bytes accessed | tf_op | source)
XLA Modules:
  0.0 335.4 jit_solution(11335868931634280589)
XLA Ops:
  7.2 0.7 and_select_fusion.1
  7.8 0.9 convert_reduce_fusion
  8.7 0.7 compare_select_fusion.1
  9.4 1.1 scatter_custom_fusion
  10.5 0.7 copy.12
  11.3 11.1 %all-to-all-start = ((s32[128,1,1]{2,1,0:T(1,128)}), s32[128,1,1]{2,1,0:T(1,128)S(1)}, u32[]{:S(2)}, u32[]{:S(2)}) async-start(s32[128,1,1]{2,1,0:T(1,128)} %copy.12), calls=%async_computation | async-start | bytes 131072 | tf_op jit(solution)/shard_map/all_to_all | solution.py:27
  22.4 3.0 scatter_custom_fusion.1
  25.4 0.5 broadcast.174
  25.9 1.4 reduce.1
  27.3 1.6 reshape.182
  28.9 2.7 all-to-all-done
  31.6 7.1 %all-to-all-start.1 = ((bf16[128,2,2048]{2,1,0:T(2,128)(2,1)}), bf16[128,2,2048]{2,1,0:T(2,128)(2,1)S(1)}, u32[]{:S(2)}, u32[]{:S(2)}) async-start(bf16[128,2,2048]{2,1,0:T(2,128)(2,1)} %reshape.182), calls=%async_computation.1 | async-start | bytes 2097152 | tf_op jit(solution)/shard_map/all_to_all | solution.py:26
  38.7 0.0 all-gather.5.cloned.1.call-start
  38.7 2.4 reduce
  41.1 16.5 %all-to-all-done.1 = bf16[128,2,2048]{2,1,0:T(2,128)(2,1)S(1)} async-done(((bf16[128,2,2048]{2,1,0:T(2,128)(2,1)}), bf16[128,2,2048]{2,1,0:T(2,128)(2,1)S(1)}, u32[]{:S(2)}, u32[]{:S(2)}) %all-to-all-start.1) | async-done | bytes 1048608 | tf_op jit(solution)/shard_map/all_to_all | solution.py:26
  57.6 1.0 reshape.183
  58.7 4.1 %scatter_custom_fusion.2 = bf16[128,4096]{1,0:T(8,128)(2,1)} fusion(s32[128]{0:T(128)S(1)} %fusion.16, bf16[128,1,4096]{2,1,0:T(2,128)(2,1)S(1)} %reshape.183, bf16[]{:T(256)} %constant.60.clone.1), kind=kCustom, calls=%fused_computation.10 | custom fusion | bytes 3145730 | tf_op jit(solution)/shard_map/scatter | solution.py:30
  62.8 0.0 all-gather.5.cloned.1.call-update
  62.8 0.2 all-gather.3.cloned.1.call-start
  63.0 0.5 all-gather.3.cloned.1.call-update
  63.6 103.0 %all-gather.5.cloned.1.call-done = bf16[1024,4096]{1,0:T(8,128)(2,1)} async-done(((bf16[128,4096]{1,0:T(8,128)(2,1)}), bf16[1024,4096]{1,0:T(8,128)(2,1)}) %all-gather.5.cloned.1.call-update) | async-done | bytes 8388624 | tf_op jit(solution)/shard_map/all_gather | solution.py:33
  166.6 5.1 %multiply_reduce_fusion.1 = f32[1024]{0:T(1024)S(1)} fusion(bf16[1024,4096]{1,0:T(8,128)(2,1)} %all-gather.5.cloned.1.call-done), kind=kLoop, calls=%fused_computation.4 | loop fusion | flops 12581888 | bytes 8392704 | tf_op jit(solution)/shard_map/reduce_sum | solution.py:9
  171.7 86.5 %all-gather.3.cloned.1.call-done = bf16[2048,4096]{1,0:T(8,128)(2,1)} async-done(((bf16[128,4096]{1,0:T(8,128)(2,1)}), bf16[2048,4096]{1,0:T(8,128)(2,1)}) %all-gather.3.cloned.1.call-update) | async-done | bytes 16777232 | tf_op jit(solution)/shard_map/all_gather | solution.py:31
  258.2 0.0 copy-start
  258.2 7.5 %multiply_reduce_fusion = f32[2048]{0:T(1024)S(1)} fusion(bf16[2048,4096]{1,0:T(8,128)(2,1)} %all-gather.3.cloned.1.call-done), kind=kLoop, calls=%fused_computation.3 | loop fusion | flops 25163776 | bytes 16785408 | tf_op jit(solution)/shard_map/reduce_sum | solution.py:9
  265.7 3.1 copy-done
  268.8 22.5 %select_reduce_fusion = (f32[2048]{0:T(1024)S(1)}, bf16[2048,1024]{0,1:T(8,128)(2,1)}) fusion(s32[1024]{0:T(1024)S(1)} %fusion.8, f32[1024]{0:T(1024)S(1)} %add_rsqrt_fusion.1, f32[2048]{0:T(1024)S(1)} %add_rsqrt_fusion, pred[1024]{0:T(1024)(128)(4,1)S(1)} %fusion.10, bf16[2048,4096]{1,0:T(8,128)(2,1)S(1)} %copy-done, ...), kind=kOutput, calls=%fused_computation.5 | convolution fusion | flops 17194547200 | bytes 29385728 | tf_op jit(solution)/shard_map/dot_general | solution.py:34
  291.3 30.9 %pmax.7 = f32[2048]{0:T(1024)} all-reduce(f32[2048]{0:T(1024)S(1)} %get-tuple-element.12), channel_id=1, replica_groups=mesh['gr'=8,'gc'=16] {'gc'}, use_global_device_ids=true, to_apply=%region_7.8 | all-reduce | flops 2048 | bytes 16384 | tf_op jit(solution)/shard_map/pmax | solution.py:44
  322.2 6.4 %copy.14 = bf16[2048,1024]{1,0:T(8,128)(2,1)} copy(bf16[2048,1024]{0,1:T(8,128)(2,1)} %get-tuple-element.13) | data formatting | bytes 8388608
  (5 shorter events, 0.0 us)
Async XLA Ops:
  11.3 20.3 %all-to-all-start = ((s32[128,1,1]{2,1,0:T(1,128)}), s32[128,1,1]{2,1,0:T(1,128)S(1)}, u32[]{:S(2)}, u32[]{:S(2)}) async-start(s32[128,1,1]{2,1,0:T(1,128)} %copy.12), calls=%async_computation | async-start | bytes 131072 | tf_op jit(solution)/shard_map/all_to_all | solution.py:27
  31.6 26.0 %all-to-all-start.1 = ((bf16[128,2,2048]{2,1,0:T(2,128)(2,1)}), bf16[128,2,2048]{2,1,0:T(2,128)(2,1)S(1)}, u32[]{:S(2)}, u32[]{:S(2)}) async-start(bf16[128,2,2048]{2,1,0:T(2,128)(2,1)} %reshape.182), calls=%async_computation.1 | async-start | bytes 2097152 | tf_op jit(solution)/shard_map/all_to_all | solution.py:26
  38.7 127.9 %all-gather.5.cloned.1.call-start = ((), (), s32[]{:S(2)}) async-start(), calls=%async_computation.3 | async-start | bytes 9437184 | tf_op jit(solution)/shard_map/all_gather | solution.py:33
  62.8 195.4 %all-gather.3.cloned.1.call-start = ((), (), s32[]{:S(2)}) async-start(), calls=%async_computation.2 | async-start | bytes 17825792 | tf_op jit(solution)/shard_map/all_gather | solution.py:31
  258.2 10.7 %copy-start = (bf16[2048,4096]{1,0:T(8,128)(2,1)S(1)}, bf16[2048,4096]{1,0:T(8,128)(2,1)}, u32[]{:S(2)}) copy-start(bf16[2048,4096]{1,0:T(8,128)(2,1)} %all-gather.3.cloned.1.call-done) | copy-start | bytes 50331652
Sparse Core Ops, SparseCore 0:
  62.9 103.5 all-gather.4
  168.8 89.2 all-gather.2
where the time goes:
time: 336 us; the launch traced here: 335 us
  waiting for transfers between devices  209 us (62%)
  blocking collectives  30.9 us (9%)
  matrix products  22.5 us (7%)
  local copies, waits for them, and re-layouts  21.6 us (6%)
  other arithmetic  18.6 us (6%)
  starting transfers between devices  18.5 us (6%)
  between operations  14.1 us (4%)
    all_gather x1, waiting for transfers between devices, per_device(): piece = lax.all_gather(local, 'gr', axis=0, tiled=True)  103 us
    all_gather x1, waiting for transfers between devices, per_device(): rows = lax.all_gather(local, 'gc', axis=0, tiled=True)  86.5 us
    pmax x1, blocking collectives, per_device(): best = lax.pmax(jnp.max(masked, axis=1), 'gc')  30.9 us
    dot_general x1, matrix products, per_device(): lax.dot_general(rows, piece, (((1,), (1,)), ((), ())), preferred_element_...  22.5 us
    all_to_all x1, waiting for transfers between devices, per_device(): lax.all_to_all(send, ('gr', 'gc'), split_axis=0, concat_axis=0, tiled=True)  16.5 us
    reduce_sum x2, other arithmetic, inverse_norm(): return 1.0 / jnp.sqrt(jnp.sum(wide * wide, axis=1) + 1e-06)  12.6 us
    unnamed x5, local copies, waits for them, and re-layouts  12.1 us
    all_to_all x1, starting transfers between devices, per_device(): lax.all_to_all(send_pos, ('gr', 'gc'), split_axis=0, concat_axis=0, tiled...  11.1 us
  transfers between devices with their start and end apart: 4, of which 4 were waited for; matrix products, arithmetic and copies ran while one was open for 4% of the time, Pallas kernels for 0%

commit v1 on v0

--- a/solution.py
+++ b/solution.py
@@ -28,7 +28,15 @@
     )
     target = jnp.where(arrived_pos >= 0, arrived_pos % count, count)
     local = jnp.zeros_like(items).at[target].set(arrived, mode="drop")
-    rows = lax.all_gather(local, "gc", axis=0, tiled=True)
+
+    def close_scales(obj):
+        everything = lax.axis_size("gc")
+        all_rows = lax.all_to_all(
+            jnp.stack([obj] * everything, axis=0), axis_name="gc", split_axis=0, concat_axis=0
+        )
+        return jnp.concatenate(all_rows, 0)
+
+    rows = close_scales(local)
     row_inv = inverse_norm(rows)
     piece = lax.all_gather(local, "gr", axis=0, tiled=True)
     product = lax.dot_general(

time: 336 us -> 420 us (1.25)
  waiting for transfers between devices: 209 us -> 286 us
  starting transfers between devices: 18.5 us -> 23.6 us
    all_gather x1, waiting for transfers between devices: 103 us -> 208 us  [per_device(): piece = lax.all_gather(local, 'gr', axis=0, tiled=True)]
    all_gather x1 -> x0, waiting for transfers between devices: 86.5 us -> none  [per_device(): rows = lax.all_gather(local, 'gc', axis=0, tiled=True)]
    all_to_all x0 -> x1, waiting for transfers between devices: none -> 57.5 us  [close_scales(): lax.all_to_all(jnp.stack([obj] * everything, axis=0), axis_name='gc', spl...]
    another operation x0 -> x1, local copies, waits for them, and re-layouts: none -> 6.17 us  [close_scales(): jnp.stack([obj] * everything, axis=0)]
    all_to_all x0 -> x1, starting transfers between devices: none -> 5.16 us  [close_scales(): lax.all_to_all(jnp.stack([obj] * everything, axis=0), axis_name='gc', spl...]
  transfers between devices with their start and end apart: 4 -> 4, of which waited for: 4 -> 4; matrix products, arithmetic and copies ran while one was open for 4% -> 3% of each run, Pallas kernels for 0% -> 0%
where the time goes in v1:
time: 420 us; the launch traced here: 419 us
  waiting for transfers between devices  286 us (68%)
  blocking collectives  28.2 us (7%)
  matrix products  25.1 us (6%)
  local copies, waits for them, and re-layouts  23.9 us (6%)
  starting transfers between devices  23.6 us (6%)
  other arithmetic  18.3 us (4%)
  between operations  14.1 us (3%)
    all_gather x1, waiting for transfers between devices, per_device(): piece = lax.all_gather(local, 'gr', axis=0, tiled=True)  208 us
    all_to_all x1, waiting for transfers between devices, close_scales(): lax.all_to_all(jnp.stack([obj] * everything, axis=0), axis_name='gc', spl...  57.5 us
    pmax x1, blocking collectives, per_device(): best = lax.pmax(jnp.max(masked, axis=1), 'gc')  28.2 us
    dot_general x1, matrix products, per_device(): lax.dot_general(rows, piece, (((1,), (1,)), ((), ())), preferred_element_...  25.1 us
    all_to_all x1, waiting for transfers between devices, per_device(): lax.all_to_all(send, ('gr', 'gc'), split_axis=0, concat_axis=0, tiled=True)  16.6 us
    reduce_sum x2, other arithmetic, inverse_norm(): return 1.0 / jnp.sqrt(jnp.sum(wide * wide, axis=1) + 1e-06)  12.3 us
    all_to_all x1, starting transfers between devices, per_device(): lax.all_to_all(send_pos, ('gr', 'gc'), split_axis=0, concat_axis=0, tiled...  11.1 us
    unnamed x5, local copies, waits for them, and re-layouts  9.03 us
  transfers between devices with their start and end apart: 4, of which 4 were waited for; matrix products, arithmetic and copies ran while one was open for 3% of the time, Pallas kernels for 0%

profile of v1, /device:TPU:0, one launch (start us, length us, event | category | flops | bytes accessed | tf_op | source)
XLA Modules:
  0.0 418.8 jit_solution(4130195910709178444)
XLA Ops:
  7.2 0.7 and_select_fusion.1
  7.8 0.9 convert_reduce_fusion
  8.7 0.7 compare_select_fusion.1
  9.4 1.1 scatter_custom_fusion
  10.5 0.7 copy.12
  11.3 11.1 %all-to-all-start = ((s32[128,1,1]{2,1,0:T(1,128)}), s32[128,1,1]{2,1,0:T(1,128)S(1)}, u32[]{:S(2)}, u32[]{:S(2)}) async-start(s32[128,1,1]{2,1,0:T(1,128)} %copy.12), calls=%async_computation | async-start | bytes 131072 | tf_op jit(solution)/shard_map/all_to_all | solution.py:27
  22.4 3.0 scatter_custom_fusion.1
  25.4 0.5 broadcast.178
  25.9 1.4 reduce.2
  27.3 1.6 reshape.195
  28.9 2.7 all-to-all-done
  31.6 7.1 %all-to-all-start.1 = ((bf16[128,2,2048]{2,1,0:T(2,128)(2,1)}), bf16[128,2,2048]{2,1,0:T(2,128)(2,1)S(1)}, u32[]{:S(2)}, u32[]{:S(2)}) async-start(bf16[128,2,2048]{2,1,0:T(2,128)(2,1)} %reshape.195), calls=%async_computation.1 | async-start | bytes 2097152 | tf_op jit(solution)/shard_map/all_to_all | solution.py:26
  38.7 2.4 reduce.1
  41.1 16.6 %all-to-all-done.1 = bf16[128,2,2048]{2,1,0:T(2,128)(2,1)S(1)} async-done(((bf16[128,2,2048]{2,1,0:T(2,128)(2,1)}), bf16[128,2,2048]{2,1,0:T(2,128)(2,1)S(1)}, u32[]{:S(2)}, u32[]{:S(2)}) %all-to-all-start.1) | async-done | bytes 1048608 | tf_op jit(solution)/shard_map/all_to_all | solution.py:26
  57.6 1.0 reshape.196
  58.7 3.4 scatter_custom_fusion.2
  62.1 0.0 copy-start
  62.1 6.2 %stack.2 = bf16[16,128,4096]{2,1,0:T(8,128)(2,1)} broadcast(bf16[128,4096]{1,0:T(8,128)(2,1)S(1)} %scatter_custom_fusion.2), dimensions={1,2} | broadcast | bytes 17825792 | tf_op jit(solution)/shard_map/stack | solution.py:35
  68.2 0.0 copy-done
  68.2 5.2 %all-to-all-start.2 = ((bf16[16,128,4096]{2,1,0:T(8,128)(2,1)}), bf16[16,128,4096]{2,1,0:T(8,128)(2,1)}, u32[]{:S(2)}, u32[]{:S(2)}) async-start(bf16[16,128,4096]{2,1,0:T(8,128)(2,1)} %stack.2), calls=%async_computation.2 | async-start | bytes 33554432 | tf_op jit(solution)/shard_map/all_to_all | solution.py:34
  73.4 0.2 all-gather.2.cloned.1.call-start
  73.6 0.5 all-gather.2.cloned.1.call-update
  74.2 208.2 %all-gather.2.cloned.1.call-done = bf16[1024,4096]{1,0:T(8,128)(2,1)} async-done(((bf16[128,4096]{1,0:T(8,128)(2,1)}), bf16[1024,4096]{1,0:T(8,128)(2,1)}) %all-gather.2.cloned.1.call-update) | async-done | bytes 8388624 | tf_op jit(solution)/shard_map/all_gather | solution.py:41
  282.4 5.1 %multiply_reduce_fusion.1 = f32[1024]{0:T(1024)S(1)} fusion(bf16[1024,4096]{1,0:T(8,128)(2,1)} %all-gather.2.cloned.1.call-done), kind=kLoop, calls=%fused_computation.4 | loop fusion | flops 12581888 | bytes 8392704 | tf_op jit(solution)/shard_map/reduce_sum | solution.py:9
  287.5 57.5 %all-to-all-done.2 = bf16[16,128,4096]{2,1,0:T(8,128)(2,1)} async-done(((bf16[16,128,4096]{2,1,0:T(8,128)(2,1)}), bf16[16,128,4096]{2,1,0:T(8,128)(2,1)}, u32[]{:S(2)}, u32[]{:S(2)}) %all-to-all-start.2) | async-done | bytes 16777248 | tf_op jit(solution)/shard_map/all_to_all | solution.py:34
  345.0 7.2 %multiply_reduce_fusion = f32[16,128]{1,0:T(8,128)S(1)} fusion(bf16[16,128,4096]{2,1,0:T(8,128)(2,1)} %all-to-all-done.2), kind=kLoop, calls=%fused_computation.3 | loop fusion | flops 25163776 | bytes 16785408 | tf_op jit(solution)/shard_map/reduce_sum | solution.py:9
  352.2 25.1 %select_reduce_fusion = (f32[2048]{0:T(1024)S(1)}, bf16[2048,1024]{0,1:T(8,128)(2,1)}) fusion(s32[1024]{0:T(1024)S(1)} %fusion.8, f32[1024]{0:T(1024)S(1)} %add_rsqrt_fusion, f32[2048]{0:T(1024)S(1)} %rsqrt_bitcast_fusion, pred[1024]{0:T(1024)(128)(4,1)S(1)} %fusion.10, bf16[2048,4096]{1,0:T(8,128)(2,1)} %bitcast.3, ...), kind=kOutput, calls=%fused_computation.5 | convolution fusion | flops 17194547200 | bytes 29385728 | tf_op jit(solution)/shard_map/dot_general | solution.py:42
  377.3 6.4 %copy.14 = bf16[2048,1024]{1,0:T(8,128)(2,1)} copy(bf16[2048,1024]{0,1:T(8,128)(2,1)} %get-tuple-element.13) | data formatting | bytes 8388608
  383.7 28.2 %pmax.7 = f32[2048]{0:T(1024)} all-reduce(f32[2048]{0:T(1024)S(1)} %get-tuple-element.12), channel_id=1, replica_groups=mesh['gr'=8,'gc'=16] {'gc'}, use_global_device_ids=true, to_apply=%region_7.8 | all-reduce | flops 2048 | bytes 16384 | tf_op jit(solution)/shard_map/pmax | solution.py:52
  (5 shorter events, 0.0 us)
Async XLA Ops:
  11.3 20.3 %all-to-all-start = ((s32[128,1,1]{2,1,0:T(1,128)}), s32[128,1,1]{2,1,0:T(1,128)S(1)}, u32[]{:S(2)}, u32[]{:S(2)}) async-start(s32[128,1,1]{2,1,0:T(1,128)} %copy.12), calls=%async_computation | async-start | bytes 131072 | tf_op jit(solution)/shard_map/all_to_all | solution.py:27
  31.6 26.0 %all-to-all-start.1 = ((bf16[128,2,2048]{2,1,0:T(2,128)(2,1)}), bf16[128,2,2048]{2,1,0:T(2,128)(2,1)S(1)}, u32[]{:S(2)}, u32[]{:S(2)}) async-start(bf16[128,2,2048]{2,1,0:T(2,128)(2,1)} %reshape.195), calls=%async_computation.1 | async-start | bytes 2097152 | tf_op jit(solution)/shard_map/all_to_all | solution.py:26
  62.1 6.2 %copy-start = (bf16[128,4096]{1,0:T(8,128)(2,1)}, bf16[128,4096]{1,0:T(8,128)(2,1)S(1)}, u32[]{:S(2)}) copy-start(bf16[128,4096]{1,0:T(8,128)(2,1)S(1)} %scatter_custom_fusion.2) | copy-start | bytes 3145732
  68.2 276.8 %all-to-all-start.2 = ((bf16[16,128,4096]{2,1,0:T(8,128)(2,1)}), bf16[16,128,4096]{2,1,0:T(8,128)(2,1)}, u32[]{:S(2)}, u32[]{:S(2)}) async-start(bf16[16,128,4096]{2,1,0:T(8,128)(2,1)} %stack.2), calls=%async_computation.2 | async-start | bytes 33554432 | tf_op jit(solution)/shard_map/all_to_all | solution.py:34
  73.4 209.0 %all-gather.2.cloned.1.call-start = ((), (), s32[]{:S(2)}) async-start(), calls=%async_computation.3 | async-start | bytes 9437184 | tf_op jit(solution)/shard_map/all_gather | solution.py:41
Sparse Core Ops, SparseCore 0:
  77.2 205.1 all-gather.1
